TPU v7x, 256 devices: a whole 4x4x8 slice. The times are simulated.
256 devices in a mesh: dp: 32 (over z_lo, y, core), tensor: 8 (over z_hi, x).
Axes of the slice: x: 4, y: 4, z: 8 (z_hi: 2, z_lo: 4; z = z_hi * 4 + z_lo), core: 2. Of those that a mesh axis runs over, the one named last changes fastest.
Arguments:
- activations: bfloat16 [32768, 4096], P('dp', 'tensor'), may hold values from -6 to 6
- grad_out: bfloat16 [32768, 11008], P('dp', 'tensor'), may hold values from -0.049804688 to 0.049804688
- subspace: bfloat16 [4096, 512], replicated, may hold values from -0.09375 to 0.09375
- first_moment: float32 [512, 11008], P('dp', 'tensor'), may hold values from -2 to 2
- second_moment: float32 [512, 11008], P('dp', 'tensor'), may hold values from 0.0001 to 0.001
Outputs:
- update: bfloat16 [4096, 11008], P('dp', 'tensor')
- new_first: float32 [512, 11008], P('dp', 'tensor')
- new_second: float32 [512, 11008], P('dp', 'tensor')
All inputs are finite; a program needn't handle non-finite values.
Results may differ from a plain program's by a relative error of at most 0.006.
Values may be sent and summed in bfloat16 or wider, within the bound.
A program may use at most 64 MiB of HBM per device.

v0:
```python
import jax
import jax.numpy as jnp
from jax import lax
from jax.sharding import PartitionSpec as P

STEP = 10


def local(activations, grad_out, subspace, first_moment, second_moment):
    projected = jnp.dot(
        lax.all_gather(activations, "tensor", axis=1, tiled=True),
        subspace,
        preferred_element_type=jnp.float32,
    )
    projected = projected.astype(jnp.bfloat16)
    reduced = lax.psum_scatter(
        lax.dot_general(
            projected, grad_out, (((0,), (0,)), ((), ())), preferred_element_type=jnp.float32
        ),
        "dp",
        scatter_dimension=0,
        tiled=True,
    )
    new_first = 0.9 * first_moment + 0.1 * reduced
    new_second = 0.999 * second_moment + 0.001 * reduced * reduced
    first_hat = new_first / (1.0 - 0.9**STEP)
    second_hat = new_second / (1.0 - 0.999**STEP)
    low_rank = (first_hat / (jnp.sqrt(second_hat) + 1e-08)).astype(jnp.bfloat16)
    own_count = subspace.shape[0] // lax.axis_size("dp")
    own_basis = lax.dynamic_slice_in_dim(subspace, lax.axis_index("dp") * own_count, own_count, 0)
    update = jnp.dot(
        own_basis,
        lax.all_gather(low_rank, "dp", axis=0, tiled=True),
        preferred_element_type=jnp.float32,
    ).astype(jnp.bfloat16)
    return (update, new_first, new_second)


def solution(mesh):
    in_specs = (P("dp", "tensor"), P("dp", "tensor"), P(), P("dp", "tensor"), P("dp", "tensor"))
    out_specs = (P("dp", "tensor"), P("dp", "tensor"), P("dp", "tensor"))
    return jax.shard_map(local, mesh=mesh, in_specs=in_specs, out_specs=out_specs, check_vma=False)
```

profile of v0, /device:TPU:1, one launch (start us, length us, event | category | flops | bytes accessed | tf_op | source)
XLA Modules:
  0.0 421.4 jit_solution(9515976217919976724)
XLA Ops:
  7.2 0.0 copy-start
  7.2 0.0 all-gather.3.cloned.1.call-start
  7.2 0.7 all-gather.3.cloned.1.call-update
  7.9 0.0 copy-start.1
  7.9 0.0 copy-start.2
  7.9 0.0 reduce-scatter.2.cloned.1.call-start
  8.0 188.2 %all-gather.3.cloned.1.call-done = bf16[1024,4096]{1,0:T(8,128)(2,1)} async-done(((bf16[1024,512]{1,0:T(8,128)(2,1)}), bf16[1024,4096]{1,0:T(8,128)(2,1)}) %all-gather.3.cloned.1.call-update) | async-done | bytes 8388624 | tf_op jit(solution)/shard_map/all_gather | solution.py:11
  196.2 0.0 copy-done
  196.2 12.4 %fusion = f32[512,1376]{1,0:T(8,128)} fusion(bf16[1024,1376]{0,1:T(8,128)(2,1)S(1)} %copy-done, bf16[1024,4096]{1,0:T(8,128)(2,1)} %all-gather.3.cloned.1.call-done, bf16[4096,512]{1,0:T(8,128)(2,1)} %param.7), kind=kOutput, calls=%fused_computation.2 | convolution fusion | flops 5738332160 | bytes 18219008 | tf_op jit(solution)/shard_map/dot_general | solution.py:17
  208.6 0.0 reduce-scatter.2.cloned.1.call-update
  208.6 0.0 all-gather.5.cloned.1.call-start
  208.7 139.8 %reduce-scatter.2.cloned.1.call-done = f32[16,1376]{1,0:T(8,128)} async-done(((f32[512,1376]{1,0:T(8,128)}), f32[16,1376]{1,0:T(8,128)}) %reduce-scatter.2.cloned.1.call-update) | async-done | bytes 88080 | tf_op jit(solution)/shard_map/reduce_scatter | solution.py:16
  348.5 0.0 copy-done.1
  348.5 0.0 copy-done.2
  348.5 1.6 divide_convert_fusion
  350.1 0.0 all-gather.5.cloned.1.call-update
  350.1 61.9 %all-gather.5.cloned.1.call-done = bf16[512,1376]{1,0:T(8,128)(2,1)} async-done(((bf16[16,1376]{1,0:T(8,128)(2,1)}), bf16[512,1376]{1,0:T(8,128)(2,1)}) %all-gather.5.cloned.1.call-update) | async-done | bytes 1409040 | tf_op jit(solution)/shard_map/all_gather | solution.py:33
  412.1 2.9 convolution_convert_fusion
Async XLA Ops:
  7.2 189.1 %copy-start = (bf16[1024,1376]{0,1:T(8,128)(2,1)S(1)}, bf16[1024,1376]{0,1:T(8,128)(2,1)}, u32[]{:S(2)}) copy-start(bf16[1024,1376]{0,1:T(8,128)(2,1)} %param.6) | copy-start | bytes 8454148
  7.2 189.0 %all-gather.3.cloned.1.call-start = ((), (), s32[]{:S(2)}) async-start(), calls=%async_computation.1 | async-start | bytes 9437184 | tf_op jit(solution)/shard_map/all_gather | solution.py:11
  7.9 340.6 %copy-start.1 = (f32[16,1376]{1,0:T(8,128)S(1)}, f32[16,1376]{1,0:T(8,128)}, u32[]{:S(2)}) copy-start(f32[16,1376]{1,0:T(8,128)} %param.8) | copy-start | bytes 264196
  7.9 340.6 %copy-start.2 = (f32[16,1376]{1,0:T(8,128)S(1)}, f32[16,1376]{1,0:T(8,128)}, u32[]{:S(2)}) copy-start(f32[16,1376]{1,0:T(8,128)} %param.9) | copy-start | bytes 264196
  7.9 340.5 %reduce-scatter.2.cloned.1.call-start = ((), (), s32[]{:S(2)}) async-start(), calls=%async_computation.2 | async-start | bytes 2973696 | tf_op jit(solution)/shard_map/reduce_scatter | solution.py:16
  208.6 203.4 %all-gather.5.cloned.1.call-start = ((), (), s32[]{:S(2)}) async-start(), calls=%async_computation.3 | async-start | bytes 1486848 | tf_op jit(solution)/shard_map/all_gather | solution.py:33
Sparse Core Ops, SparseCore 0:
  10.5 185.6 all-gather.2
  208.7 139.7 reduce-scatter.1
  350.9 61.0 all-gather.4
where the time goes:
time: 422 us; the launch traced here: 421 us
  waiting for transfers between devices  391 us (93%)
  matrix products  15.2 us (4%)
  between operations  13.8 us (3%)
    all_gather x1, waiting for transfers between devices, local(): lax.all_gather(activations, 'tensor', axis=1, tiled=True)  188 us
    reduce_scatter x1, waiting for transfers between devices, local(): lax.psum_scatter(lax.dot_general(projected, grad_out, (((0,), (0,)), ((),...  140 us
    all_gather x1, waiting for transfers between devices, local(): lax.all_gather(low_rank, 'dp', axis=0, tiled=True)  61.9 us
    dot_general x1, matrix products, local(): lax.dot_general(projected, grad_out, (((0,), (0,)), ((), ())), preferred_...  12.4 us
  transfers between devices with their start and end apart: 3, of which 3 were waited for; matrix products, arithmetic and copies ran while one was open for 0% of the time, Pallas kernels for 0%

commit v1 on v0

v1 whole, which is shorter than its diff:
```python
import jax
import jax.numpy as jnp
from jax import lax
from jax.experimental import pallas as pl
from jax.experimental.pallas import tpu as pltpu
from jax.sharding import PartitionSpec as P

STEP = 10
MESH = pl.DeviceIdType.MESH
NX, NY, NZ = 4, 4, 4
KC = 4

STAGE_AT = (0.0, 5.0, 11.0, 17.0, 20.0, 24.0, 27.0, 30.0, 34.0, 36.0)
CHUNK_AFTER = 3.3


def kernel(
    a_hbm, g_hbm, s_hbm, m_hbm, v_hbm,
    up_hbm, nf_hbm, ns_hbm,
    a_v, g_v, s_v, b_v, m_v, v_v,
    xs, xo, xr, ho, zs, zr, pt, rf, cs, cr, ty, ys, yr, ws, wr, lr, acc, up_v, nf_v, ns_v,
    ld, st, xss, xrs, zss, zrs, xas, xar, css, crs, yss, yrs, wss, wrs, bss, brs, yas, yar, c2s, c2r,
):
    dp = lax.axis_index("dp")
    t = lax.axis_index("tensor")
    x, zh = t % NX, t // NX
    zl, y, c = dp // 8, (dp // 2) % NY, dp % 2
    f32, bf16 = jnp.float32, jnp.bfloat16
    rank = pt.shape[0]
    kr = rank // KC
    own = kr // (2 * NY)
    tb = a_v.shape[1]
    depth = s_v.shape[0]
    rows = b_v.shape[0]

    def x_at(d):
        return (dp, zh * NX + (x + d) % NX)

    def y_at(d):
        return (zl * 8 + ((y + d) % NY) * 2 + c, t)

    def z_at(k):
        return (k * 8 + y * 2 + c, t)

    z_far = (dp, (1 - zh) * NX + x)
    core = (dp + 1 - 2 * c, t)

    barrier = pltpu.get_barrier_semaphore()
    peers = [x_at(d) for d in range(1, NX)] + [y_at(d) for d in range(1, NY)]
    peers += [z_at((zl + d) % NZ) for d in range(1, NZ)] + [z_far, core]
    for peer in peers:
        pl.semaphore_signal(barrier, inc=1, device_id=peer, device_id_type=MESH)

    loads = [pltpu.make_async_copy(s_hbm.at[pl.ds(pl.multiple_of(t * depth, depth), depth)], s_v, ld.at[0])]
    for i, d in enumerate((1, 2, 3, 0)):
        at = pl.multiple_of(((x + d) % NX) * tb, tb)
        loads.append(pltpu.make_async_copy(a_hbm.at[pl.ds(at, tb)], a_v.at[d], ld.at[1 + i]))
    for d in range(NX):
        at = pl.multiple_of(((x + NX - d) % NX) * tb, tb)
        loads.append(pltpu.make_async_copy(g_hbm.at[pl.ds(at, tb)], g_v.at[pl.ds(d * tb, tb)], ld.at[5 + d]))
    loads.append(pltpu.make_async_copy(m_hbm, m_v, ld.at[9]))
    loads.append(pltpu.make_async_copy(v_hbm, v_v, ld.at[10]))
    loads.append(pltpu.make_async_copy(s_hbm.at[pl.ds(pl.multiple_of(dp * rows, rows), rows)], b_v, ld.at[11]))
    for load in loads:
        load.start()

    def remote(src, dst, send, recv, to):
        return pltpu.make_async_remote_copy(
            src_ref=src, dst_ref=dst, send_sem=send, recv_sem=recv, device_id=to, device_id_type=MESH
        )

    def ks(k):
        return pl.ds(k * kr, kr)

    def x_copy(k, d):
        return remote(xs.at[d - 1, ks(k)], xr.at[d - 1, ks(k)], xss.at[k, d - 1], xrs.at[k, d - 1], x_at(d))

    def z_copy(k):
        return remote(zs.at[ks(k)], zr.at[ks(k)], zss.at[k], zrs.at[k], z_far)

    def xa_copy(k, d):
        return remote(
            pt.at[ks(k), pl.ds(0, tb)], pt.at[ks(k), pl.ds(d * tb, tb)], xas.at[k, d - 1], xar.at[k, d - 1], x_at(d)
        )

    def c_copy(k):
        return remote(cs.at[k], cr.at[k], css.at[k], crs.at[k], core)

    def y_copy(k, d):
        return remote(ys.at[k, (y + d) % NY], yr.at[k, d - 1], yss.at[k, d - 1], yrs.at[k, d - 1], y_at(d))

    def w_copy(k):
        slot = (zl - k + NZ - 1) % NZ
        return remote(ws.at[k], wr.at[slot], wss.at[k], wrs.at[slot], z_at(k))

    def b_copy(k, d):
        mine = lr.at[k, y, c]
        return remote(mine, mine, bss.at[d - 1], brs.at[k], z_at((k + d) % NZ))

    def ya_copy(k, d):
        mine = lr.at[k, y, c]
        return remote(mine, mine, yas.at[k, d - 1], yar.at[k, d - 1], y_at(d))

    def ya_wait(k, d):
        theirs = lr.at[k, (y + NY - d) % NY, c]
        remote(theirs, theirs, yas.at[k, d - 1], yar.at[k, d - 1], y_at(d)).wait_recv()

    def c2_copy(k):
        half = lr.at[k, :, c]
        return remote(half, half, c2s.at[k], c2r.at[k], core)

    def c2_wait(k):
        half = lr.at[k, :, 1 - c]
        remote(half, half, c2s.at[k], c2r.at[k], core).wait_recv()

    def project(k, d):
        return lax.dot_general(
            s_v[:, k * kr : (k + 1) * kr], a_v[d], (((0,), (1,)), ((), ())), preferred_element_type=f32
        )

    def stage0(k):
        for i, d in enumerate((1, 2, 3)):
            if k == 0:
                if i == 0:
                    loads[0].wait()
                loads[1 + i].wait()
            xs[d - 1, k * kr : (k + 1) * kr] = project(k, d).astype(bf16)
            if k == 0 and i == 0:
                pl.semaphore_wait(barrier, len(peers))
            x_copy(k, d).start()
        if k == 0:
            loads[4].wait()
        xo[k * kr : (k + 1) * kr] = project(k, 0)

    def stage1(k):
        r = slice(k * kr, (k + 1) * kr)
        for d in (1, 2, 3):
            x_copy(k, d).wait_recv()
        h = xo[r] + xr[0, r].astype(f32) + xr[1, r].astype(f32) + xr[2, r].astype(f32)
        zs[r] = h.astype(bf16)
        z_copy(k).start()
        ho[r] = h

    def stage2(k):
        r = slice(k * kr, (k + 1) * kr)
        z_copy(k).wait_recv()
        pt[r, 0:tb] = (ho[r] + zr[r].astype(f32)).astype(bf16)
        for d in (1, 2, 3):
            xa_copy(k, d).start()

    def stage3(k):
        for d in (1, 2, 3):
            xa_copy(k, d).wait_recv()
        if k == 0:
            for d in range(NX):
                loads[5 + d].wait()
        red = jnp.dot(pt[k * kr : (k + 1) * kr], g_v[...], preferred_element_type=f32)
        for yy in range(NY):
            for cc in range(2):
                at = (yy * 2 + cc) * own
                rf[k, cc, yy] = red[at : at + own]
        cs[k] = rf[k, 1 - c].astype(bf16)
        c_copy(k).start()

    def stage4(k):
        c_copy(k).wait_recv()
        both = rf[k, c] + cr[k].astype(f32)
        ys[k] = both.astype(bf16)
        for d in (1, 2, 3):
            y_copy(k, d).start()
        ty[k] = both

    def stage5(k):
        for d in (1, 2, 3):
            y_copy(k, d).wait_recv()
        total = ty[k, y] + yr[k, 0].astype(f32) + yr[k, 1].astype(f32) + yr[k, 2].astype(f32)
        ty[k, y] = total

        @pl.when(zl != k)
        def _():
            ws[k] = total.astype(bf16)
            w_copy(k).start()

    def stage6(k):
        @pl.when(zl == k)
        def _():
            for d in (1, 2, 3):
                remote(ws.at[k], wr.at[d - 1], wss.at[k], wrs.at[d - 1], z_at((k + d) % NZ)).wait_recv()
            loads[9].wait()
            loads[10].wait()
            reduced = ty[k, y] + wr[0].astype(f32) + wr[1].astype(f32) + wr[2].astype(f32)
            new_first = 0.9 * m_v[...] + 0.1 * reduced
            new_second = 0.999 * v_v[...] + 0.001 * reduced * reduced
            first_hat = new_first / (1.0 - 0.9**STEP)
            second_hat = new_second / (1.0 - 0.999**STEP)
            lr[k, y, c] = (first_hat / (jnp.sqrt(second_hat) + 1e-08)).astype(bf16)
            for d in (2, 1, 3):
                b_copy(k, d).start()
            nf_v[...] = new_first
            ns_v[...] = new_second
            pltpu.make_async_copy(nf_v, nf_hbm, st.at[0]).start()
            pltpu.make_async_copy(ns_v, ns_hbm, st.at[1]).start()

    def stage7(k):
        @pl.when(zl != k)
        def _():
            b_copy(k, 1).wait_recv()

        for d in (1, 2, 3):
            ya_copy(k, d).start()

    def stage8(k):
        for d in (1, 2, 3):
            ya_wait(k, d)
        c2_copy(k).start()

    def stage9(k):
        c2_wait(k)
        if k == 0:
            loads[11].wait()
        low = lr[k].reshape(kr, lr.shape[-1])
        part = jnp.dot(b_v[:, k * kr : (k + 1) * kr], low, preferred_element_type=f32)
        if k == 0:
            acc[...] = part
        elif k < KC - 1:
            acc[...] += part
        else:
            up_v[...] = (acc[...] + part).astype(bf16)
            pltpu.make_async_copy(up_v, up_hbm, st.at[2]).start()

    stages = (stage0, stage1, stage2, stage3, stage4, stage5, stage6, stage7, stage8, stage9)
    plan = [(at + (CHUNK_AFTER * k if s else 0.1 * k), k, s) for s, at in enumerate(STAGE_AT) for k in range(KC)]
    for _, k, s in sorted(plan):
        stages[s](k)

    for k in range(KC):
        for d in (1, 2, 3):
            x_copy(k, d).wait_send()
            xa_copy(k, d).wait_send()
            y_copy(k, d).wait_send()
            ya_copy(k, d).wait_send()
        z_copy(k).wait_send()
        c_copy(k).wait_send()
        c2_copy(k).wait_send()

        @pl.when(zl != k)
        def _():
            w_copy(k).wait_send()

    for d in (1, 2, 3):
        b_copy(0, d).wait_send()
    pltpu.make_async_copy(nf_v, nf_hbm, st.at[0]).wait()
    pltpu.make_async_copy(ns_v, ns_hbm, st.at[1]).wait()
    pltpu.make_async_copy(up_v, up_hbm, st.at[2]).wait()


def local(activations, grad_out, subspace, first_moment, second_moment):
    tokens, depth = activations.shape
    ff = grad_out.shape[1]
    rank = subspace.shape[1]
    own = first_moment.shape[0]
    rows = subspace.shape[0] // lax.axis_size("dp")
    tb = tokens // NX
    kr = rank // KC
    f32, bf16 = jnp.float32, jnp.bfloat16
    dma = pltpu.SemaphoreType.DMA
    anywhere = pl.BlockSpec(memory_space=pl.ANY)
    scratch = [
        ((NX, tb, depth), bf16),
        ((tokens, ff), bf16),
        ((depth, rank), bf16),
        ((rows, rank), bf16),
        ((own, ff), f32),
        ((own, ff), f32),
        ((NX - 1, rank, tb), bf16),
        ((rank, tb), f32),
        ((NX - 1, rank, tb), bf16),
        ((rank, tb), f32),
        ((rank, tb), bf16),
        ((rank, tb), bf16),
        ((rank, tokens), bf16),
        ((KC, 2, NY, own, ff), f32),
        ((KC, NY, own, ff), bf16),
        ((KC, NY, own, ff), bf16),
        ((KC, NY, own, ff), f32),
        ((KC, NY, own, ff), bf16),
        ((KC, NY - 1, own, ff), bf16),
        ((KC, own, ff), bf16),
        ((NZ - 1, own, ff), bf16),
        ((KC, NY, 2, own, ff), bf16),
        ((rows, ff), f32),
        ((rows, ff), bf16),
        ((own, ff), f32),
        ((own, ff), f32),
    ]
    sems = [(12,), (3,), (KC, 3), (KC, 3), (KC,), (KC,), (KC, 3), (KC, 3), (KC,), (KC,), (KC, 3), (KC, 3)]
    sems += [(KC,), (3,), (3,), (KC,), (KC, 3), (KC, 3), (KC,), (KC,)]
    flops = 2 * tokens * rank * (depth + ff) + 2 * rows * rank * ff
    return pl.pallas_call(
        kernel,
        out_shape=(
            jax.ShapeDtypeStruct((rows, ff), bf16),
            jax.ShapeDtypeStruct((own, ff), f32),
            jax.ShapeDtypeStruct((own, ff), f32),
        ),
        in_specs=[anywhere] * 5,
        out_specs=(anywhere,) * 3,
        scratch_shapes=[pltpu.VMEM(shape, dtype) for shape, dtype in scratch] + [dma(shape) for shape in sems],
        compiler_params=pltpu.CompilerParams(collective_id=0, has_side_effects=True, vmem_limit_bytes=56 << 20),
        cost_estimate=pl.CostEstimate(flops=flops, bytes_accessed=8 << 20, transcendentals=own * ff),
        name="galore",
    )(activations, grad_out, subspace, first_moment, second_moment)


def solution(mesh):
    in_specs = (P("dp", "tensor"), P("dp", "tensor"), P(), P("dp", "tensor"), P("dp", "tensor"))
    out_specs = (P("dp", "tensor"), P("dp", "tensor"), P("dp", "tensor"))
    return jax.shard_map(local, mesh=mesh, in_specs=in_specs, out_specs=out_specs, check_vma=False)
```

time: 422 us -> 76.5 us (0.18)
  waiting for transfers between devices: 391 us -> 0 us
  Pallas kernels: 0 us -> 66.1 us
  matrix products: 15.2 us -> 0 us
  between operations: 13.8 us -> 0.64 us
  local copies, waits for them, and re-layouts: 0.02 us -> 9.53 us
    all_gather x2 -> x0, waiting for transfers between devices: 250 us -> none  [the longest x1 188 us: local(): lax.all_gather(activations, 'tensor', axis=1, tiled=True)]
    reduce_scatter x1 -> x0, waiting for transfers between devices: 140 us -> none  [local(): lax.psum_scatter(lax.dot_general(projected, grad_out, (((0,), (0,)), ((),...]
    pallas_call x0 -> x1, Pallas kernels: none -> 66.1 us  [local(): pl.pallas_call(kernel, out_shape=(jax.ShapeDtypeStruct((rows, ff), bf16),...]
    dot_general x2 -> x0, matrix products: 15.2 us -> none  [the longest x1 12.4 us: local(): lax.dot_general(projected, grad_out, (((0,), (0,)), ((), ())), preferred_...]
    unnamed x6 -> x3, local copies, waits for them, and re-layouts: 0.02 us -> 7.64 us
  transfers between devices with their start and end apart: 3 -> 0, of which waited for: 3 -> 0; matrix products, arithmetic and copies ran while one was open for 0% -> 0% of each run, Pallas kernels for 0% -> 0%
where the time goes in v1:
time: 76.5 us; the launch traced here: 76.2 us
  Pallas kernels  66.1 us (86%)
  local copies, waits for them, and re-layouts  9.53 us (12%)
    pallas_call x1, Pallas kernels, local(): pl.pallas_call(kernel, out_shape=(jax.ShapeDtypeStruct((rows, ff), bf16),...  66.1 us
    unnamed x3, local copies, waits for them, and re-layouts  7.64 us
    pallas_call x1, local copies, waits for them, and re-layouts, local(): pl.pallas_call(kernel, out_shape=(jax.ShapeDtypeStruct((rows, ff), bf16),...  1.89 us

profile of v1, /device:TPU:1, one launch (start us, length us, event | category | flops | bytes accessed | tf_op | source)
XLA Modules:
  0.0 76.2 jit_solution(10310810107160916514)
XLA Ops:
  0.6 4.6 %copy.8.g_hbm = bf16[1024,1376]{1,0:T(8,128)(2,1)} copy(bf16[1024,1376]{0,1:T(8,128)(2,1)} %param.6) | data formatting | bytes 5636096 | tf_op args[1]
  5.2 66.1 %galore.1 = (bf16[128,1376]{1,0:T(8,128)(2,1)}, f32[16,1376]{1,0:T(8,128)}, f32[16,1376]{1,0:T(8,128)}) custom-call(bf16[1024,512]{1,0:T(8,128)(2,1)} %a_hbm.1, bf16[1024,1376]{1,0:T(8,128)(2,1)} %copy.8.g_hbm, bf16[4096,512]{1,0:T(8,128)(2,1)} %s_hbm.1, f32[16,1376]{1,0:T(8,128)} %m_hbm.1, f32[16,1376]{1,0:T(8,128)} %v_hbm.1), custom_call_target="tpu_custom_call" | custom-call | flops 2160066560 | bytes 8388608 | tf_op jit(solution)/shard_map/galore/pallas_call | solution.py:299
  71.3 1.9 %copy.9 = bf16[128,1376]{0,1:T(8,128)(2,1)} copy(bf16[128,1376]{1,0:T(8,128)(2,1)} %get-tuple-element.3) | data formatting | bytes 704512 | tf_op jit(solution)/shard_map/galore/pallas_call | solution.py:299
  73.2 1.5 %copy.12 = f32[16,1376]{1,0:T(8,128)} copy(f32[16,1376]{1,0:T(8,128)} %get-tuple-element.10) | data formatting | bytes 176128
  74.7 1.5 %copy.13 = f32[16,1376]{1,0:T(8,128)} copy(f32[16,1376]{1,0:T(8,128)} %get-tuple-element.11) | data formatting | bytes 176128

commit v2 on v1

--- a/solution.py
+++ b/solution.py
@@ -11,13 +11,19 @@
 KC = 4
 
 STAGE_AT = (0.0, 5.0, 11.0, 17.0, 20.0, 24.0, 27.0, 30.0, 34.0, 36.0)
-CHUNK_AFTER = 3.3
+CHUNK_AFTER = 2.0
+TURN = (0, 3, 1, 2)
+
+
+def order():
+    plan = [(at + (CHUNK_AFTER * i if s else 0.1 * i), i, s) for s, at in enumerate(STAGE_AT) for i in range(KC)]
+    return [(TURN[i], s) for _, i, s in sorted(plan)]
 
 
 def kernel(
     a_hbm, g_hbm, s_hbm, m_hbm, v_hbm,
     up_hbm, nf_hbm, ns_hbm,
-    a_v, g_v, s_v, b_v, m_v, v_v,
+    a_v, g_v, gt, s_v, b_v, m_v, v_v,
     xs, xo, xr, ho, zs, zr, pt, rf, cs, cr, ty, ys, yr, ws, wr, lr, acc, up_v, nf_v, ns_v,
     ld, st, xss, xrs, zss, zrs, xas, xar, css, crs, yss, yrs, wss, wrs, bss, brs, yas, yar, c2s, c2r,
 ):
@@ -57,7 +63,7 @@
         loads.append(pltpu.make_async_copy(a_hbm.at[pl.ds(at, tb)], a_v.at[d], ld.at[1 + i]))
     for d in range(NX):
         at = pl.multiple_of(((x + NX - d) % NX) * tb, tb)
-        loads.append(pltpu.make_async_copy(g_hbm.at[pl.ds(at, tb)], g_v.at[pl.ds(d * tb, tb)], ld.at[5 + d]))
+        loads.append(pltpu.make_async_copy(g_hbm.at[:, pl.ds(at, tb)], g_v.at[:, pl.ds(d * tb, tb)], ld.at[5 + d]))
     loads.append(pltpu.make_async_copy(m_hbm, m_v, ld.at[9]))
     loads.append(pltpu.make_async_copy(v_hbm, v_v, ld.at[10]))
     loads.append(pltpu.make_async_copy(s_hbm.at[pl.ds(pl.multiple_of(dp * rows, rows), rows)], b_v, ld.at[11]))
@@ -69,6 +75,9 @@
             src_ref=src, dst_ref=dst, send_sem=send, recv_sem=recv, device_id=to, device_id_type=MESH
         )
 
+    def far_first(k):
+        return sorted((1, 2, 3), key=lambda d: -abs((k + d) % NZ - k))
+
     def ks(k):
         return pl.ds(k * kr, kr)
 
@@ -105,13 +114,13 @@
         theirs = lr.at[k, (y + NY - d) % NY, c]
         remote(theirs, theirs, yas.at[k, d - 1], yar.at[k, d - 1], y_at(d)).wait_recv()
 
-    def c2_copy(k):
-        half = lr.at[k, :, c]
-        return remote(half, half, c2s.at[k], c2r.at[k], core)
-
-    def c2_wait(k):
-        half = lr.at[k, :, 1 - c]
-        remote(half, half, c2s.at[k], c2r.at[k], core).wait_recv()
+    def c2_copy(k, d):
+        piece = lr.at[k, (y + NY - d) % NY, c]
+        return remote(piece, piece, c2s.at[k, d], c2r.at[k, d], core)
+
+    def c2_wait(k, d):
+        piece = lr.at[k, (y + NY - d) % NY, 1 - c]
+        remote(piece, piece, c2s.at[k, d], c2r.at[k, d], core).wait_recv()
 
     def project(k, d):
         return lax.dot_general(
@@ -120,41 +129,49 @@
 
     def stage0(k):
         for i, d in enumerate((1, 2, 3)):
-            if k == 0:
+            if k == TURN[0]:
                 if i == 0:
                     loads[0].wait()
                 loads[1 + i].wait()
             xs[d - 1, k * kr : (k + 1) * kr] = project(k, d).astype(bf16)
-            if k == 0 and i == 0:
+            if k == TURN[0] and i == 0:
                 pl.semaphore_wait(barrier, len(peers))
             x_copy(k, d).start()
-        if k == 0:
+        if k == TURN[0]:
             loads[4].wait()
         xo[k * kr : (k + 1) * kr] = project(k, 0)
 
+    def wait1(k):
+        for d in (1, 2, 3):
+            x_copy(k, d).wait_recv()
+
     def stage1(k):
         r = slice(k * kr, (k + 1) * kr)
-        for d in (1, 2, 3):
-            x_copy(k, d).wait_recv()
         h = xo[r] + xr[0, r].astype(f32) + xr[1, r].astype(f32) + xr[2, r].astype(f32)
         zs[r] = h.astype(bf16)
         z_copy(k).start()
         ho[r] = h
 
+    def wait2(k):
+        z_copy(k).wait_recv()
+
     def stage2(k):
         r = slice(k * kr, (k + 1) * kr)
-        z_copy(k).wait_recv()
         pt[r, 0:tb] = (ho[r] + zr[r].astype(f32)).astype(bf16)
         for d in (1, 2, 3):
             xa_copy(k, d).start()
 
+    def wait3(k):
+        for d in (1, 2, 3):
+            xa_copy(k, d).wait_recv()
+
+    def turn_g():
+        for d in range(NX):
+            loads[5 + d].wait()
+            gt[d * tb : (d + 1) * tb] = g_v[:, d * tb : (d + 1) * tb].T
+
     def stage3(k):
-        for d in (1, 2, 3):
-            xa_copy(k, d).wait_recv()
-        if k == 0:
-            for d in range(NX):
-                loads[5 + d].wait()
-        red = jnp.dot(pt[k * kr : (k + 1) * kr], g_v[...], preferred_element_type=f32)
+        red = jnp.dot(pt[k * kr : (k + 1) * kr], gt[...], preferred_element_type=f32)
         for yy in range(NY):
             for cc in range(2):
                 at = (yy * 2 + cc) * own
@@ -162,17 +179,21 @@
         cs[k] = rf[k, 1 - c].astype(bf16)
         c_copy(k).start()
 
+    def wait4(k):
+        c_copy(k).wait_recv()
+
     def stage4(k):
-        c_copy(k).wait_recv()
         both = rf[k, c] + cr[k].astype(f32)
         ys[k] = both.astype(bf16)
         for d in (1, 2, 3):
             y_copy(k, d).start()
         ty[k] = both
 
+    def wait5(k):
+        for d in (1, 2, 3):
+            y_copy(k, d).wait_recv()
+
     def stage5(k):
-        for d in (1, 2, 3):
-            y_copy(k, d).wait_recv()
         total = ty[k, y] + yr[k, 0].astype(f32) + yr[k, 1].astype(f32) + yr[k, 2].astype(f32)
         ty[k, y] = total
 
@@ -181,11 +202,15 @@
             ws[k] = total.astype(bf16)
             w_copy(k).start()
 
+    def wait6(k):
+        @pl.when(zl == k)
+        def _():
+            for d in (1, 2, 3):
+                remote(ws.at[k], wr.at[d - 1], wss.at[k], wrs.at[d - 1], z_at((k + d) % NZ)).wait_recv()
+
     def stage6(k):
         @pl.when(zl == k)
         def _():
-            for d in (1, 2, 3):
-                remote(ws.at[k], wr.at[d - 1], wss.at[k], wrs.at[d - 1], z_at((k + d) % NZ)).wait_recv()
             loads[9].wait()
             loads[10].wait()
             reduced = ty[k, y] + wr[0].astype(f32) + wr[1].astype(f32) + wr[2].astype(f32)
@@ -194,44 +219,58 @@
             first_hat = new_first / (1.0 - 0.9**STEP)
             second_hat = new_second / (1.0 - 0.999**STEP)
             lr[k, y, c] = (first_hat / (jnp.sqrt(second_hat) + 1e-08)).astype(bf16)
-            for d in (2, 1, 3):
+            for d in far_first(k):
                 b_copy(k, d).start()
             nf_v[...] = new_first
             ns_v[...] = new_second
             pltpu.make_async_copy(nf_v, nf_hbm, st.at[0]).start()
             pltpu.make_async_copy(ns_v, ns_hbm, st.at[1]).start()
 
+    def wait7(k):
+        @pl.when(zl != k)
+        def _():
+            b_copy(k, 1).wait_recv()
+
     def stage7(k):
-        @pl.when(zl != k)
-        def _():
-            b_copy(k, 1).wait_recv()
-
-        for d in (1, 2, 3):
+        for d in (2, 1, 3):
             ya_copy(k, d).start()
+        c2_copy(k, 0).start()
+
+    def wait8(k):
+        for d in (1, 3, 2):
+            ya_wait(k, d)
+            c2_copy(k, d).start()
 
     def stage8(k):
-        for d in (1, 2, 3):
-            ya_wait(k, d)
-        c2_copy(k).start()
+        pass
+
+    def wait9(k):
+        for d in (0, 1, 3, 2):
+            c2_wait(k, d)
 
     def stage9(k):
-        c2_wait(k)
-        if k == 0:
+        if k == TURN[0]:
             loads[11].wait()
         low = lr[k].reshape(kr, lr.shape[-1])
-        part = jnp.dot(b_v[:, k * kr : (k + 1) * kr], low, preferred_element_type=f32)
-        if k == 0:
+        part = lax.dot_general(
+            low, b_v[:, k * kr : (k + 1) * kr], (((0,), (1,)), ((), ())), preferred_element_type=f32
+        )
+        if k == TURN[0]:
             acc[...] = part
-        elif k < KC - 1:
+        elif k != TURN[-1]:
             acc[...] += part
         else:
             up_v[...] = (acc[...] + part).astype(bf16)
             pltpu.make_async_copy(up_v, up_hbm, st.at[2]).start()
 
+    waits = (None, wait1, wait2, wait3, wait4, wait5, wait6, wait7, wait8, wait9)
     stages = (stage0, stage1, stage2, stage3, stage4, stage5, stage6, stage7, stage8, stage9)
-    plan = [(at + (CHUNK_AFTER * k if s else 0.1 * k), k, s) for s, at in enumerate(STAGE_AT) for k in range(KC)]
-    for _, k, s in sorted(plan):
+    for k, s in order():
+        if waits[s]:
+            waits[s](k)
         stages[s](k)
+        if (k, s) == (TURN[-1], 0):
+            turn_g()
 
     for k in range(KC):
         for d in (1, 2, 3):
@@ -241,7 +280,8 @@
             ya_copy(k, d).wait_send()
         z_copy(k).wait_send()
         c_copy(k).wait_send()
-        c2_copy(k).wait_send()
+        for d in range(NY):
+            c2_copy(k, d).wait_send()
 
         @pl.when(zl != k)
         def _():
@@ -252,6 +292,19 @@
     pltpu.make_async_copy(nf_v, nf_hbm, st.at[0]).wait()
     pltpu.make_async_copy(ns_v, ns_hbm, st.at[1]).wait()
     pltpu.make_async_copy(up_v, up_hbm, st.at[2]).wait()
+
+
+def hand_on(up_in, nf_in, ns_in, up_out, nf_out, ns_out, up_v, nf_v, ns_v, sem):
+    trips = ((nf_in, nf_v, nf_out), (ns_in, ns_v, ns_out), (up_in, up_v, up_out))
+    reads = [pltpu.make_async_copy(src, via, sem.at[0, i]) for i, (src, via, _) in enumerate(trips)]
+    writes = [pltpu.make_async_copy(via, dst, sem.at[1, i]) for i, (_, via, dst) in enumerate(trips)]
+    for read in reads:
+        read.start()
+    for read, write in zip(reads, writes):
+        read.wait()
+        write.start()
+    for write in writes:
+        write.wait()
 
 
 def local(activations, grad_out, subspace, first_moment, second_moment):
@@ -267,6 +320,7 @@
     anywhere = pl.BlockSpec(memory_space=pl.ANY)
     scratch = [
         ((NX, tb, depth), bf16),
+        ((ff, tokens), bf16),
         ((tokens, ff), bf16),
         ((depth, rank), bf16),
         ((rows, rank), bf16),
@@ -288,28 +342,39 @@
         ((KC, own, ff), bf16),
         ((NZ - 1, own, ff), bf16),
         ((KC, NY, 2, own, ff), bf16),
-        ((rows, ff), f32),
-        ((rows, ff), bf16),
+        ((ff, rows), f32),
+        ((ff, rows), bf16),
         ((own, ff), f32),
         ((own, ff), f32),
     ]
     sems = [(12,), (3,), (KC, 3), (KC, 3), (KC,), (KC,), (KC, 3), (KC, 3), (KC,), (KC,), (KC, 3), (KC, 3)]
-    sems += [(KC,), (3,), (3,), (KC,), (KC, 3), (KC, 3), (KC,), (KC,)]
+    sems += [(KC,), (3,), (3,), (KC,), (KC, 3), (KC, 3), (KC, NY), (KC, NY)]
     flops = 2 * tokens * rank * (depth + ff) + 2 * rows * rank * ff
-    return pl.pallas_call(
+    shapes = (
+        jax.ShapeDtypeStruct((ff, rows), bf16),
+        jax.ShapeDtypeStruct((own, ff), f32),
+        jax.ShapeDtypeStruct((own, ff), f32),
+    )
+    made = pl.pallas_call(
         kernel,
-        out_shape=(
-            jax.ShapeDtypeStruct((rows, ff), bf16),
-            jax.ShapeDtypeStruct((own, ff), f32),
-            jax.ShapeDtypeStruct((own, ff), f32),
-        ),
+        out_shape=shapes,
         in_specs=[anywhere] * 5,
         out_specs=(anywhere,) * 3,
         scratch_shapes=[pltpu.VMEM(shape, dtype) for shape, dtype in scratch] + [dma(shape) for shape in sems],
         compiler_params=pltpu.CompilerParams(collective_id=0, has_side_effects=True, vmem_limit_bytes=56 << 20),
         cost_estimate=pl.CostEstimate(flops=flops, bytes_accessed=8 << 20, transcendentals=own * ff),
         name="galore",
-    )(activations, grad_out, subspace, first_moment, second_moment)
+    )(activations, grad_out.T, subspace, first_moment, second_moment)
+    update, new_first, new_second = pl.pallas_call(
+        hand_on,
+        out_shape=shapes,
+        in_specs=[anywhere] * 3,
+        out_specs=(anywhere,) * 3,
+        scratch_shapes=[pltpu.VMEM(made.shape, made.dtype) for made in shapes] + [dma((2, 3))],
+        compiler_params=pltpu.CompilerParams(vmem_limit_bytes=56 << 20),
+        name="hand_on",
+    )(*made)
+    return update.T, new_first, new_second
 
 
 def solution(mesh):

time: 76.5 us -> 63.2 us (0.83)
  local copies, waits for them, and re-layouts: 9.53 us -> 0 us
  Pallas kernels: 66.1 us -> 62.4 us
    unnamed x3 -> x0, local copies, waits for them, and re-layouts: 7.64 us -> none
    pallas_call x1 -> x2, Pallas kernels: 66.1 us -> 62.4 us  [the longest x1 60.6 us: local(): pl.pallas_call(kernel, out_shape=shapes, in_specs=[anywhere] * 5, out_spe...]
    pallas_call x1 -> x0, local copies, waits for them, and re-layouts: 1.89 us -> none  [local(): pl.pallas_call(kernel, out_shape=(jax.ShapeDtypeStruct((rows, ff), bf16),...]
where the time goes in v2:
time: 63.2 us; the launch traced here: 63.1 us
  Pallas kernels  62.4 us (99%)
  between operations  0.64 us (1%)
    pallas_call x1, Pallas kernels, local(): pl.pallas_call(kernel, out_shape=shapes, in_specs=[anywhere] * 5, out_spe...  60.6 us
    pallas_call x1, Pallas kernels, local(): pl.pallas_call(hand_on, out_shape=shapes, in_specs=[anywhere] * 3, out_sp...  1.86 us

profile of v2, /device:TPU:1, one launch (start us, length us, event | category | flops | bytes accessed | tf_op | source)
XLA Modules:
  0.0 63.1 jit_solution(1227949425254563838)
XLA Ops:
  0.6 60.6 %galore.1 = (bf16[1376,128]{1,0:T(8,128)(2,1)}, f32[16,1376]{1,0:T(8,128)}, f32[16,1376]{1,0:T(8,128)}) custom-call(bf16[1024,512]{1,0:T(8,128)(2,1)} %a_hbm.1, bf16[1376,1024]{1,0:T(8,128)(2,1)} %bitcast.2, bf16[4096,512]{1,0:T(8,128)(2,1)} %s_hbm.1, f32[16,1376]{1,0:T(8,128)} %m_hbm.1, f32[16,1376]{1,0:T(8,128)} %v_hbm.1), custom_call_target="tpu_custom_call" | custom-call | flops 2160066560 | bytes 8388608 | tf_op jit(solution)/shard_map/galore/pallas_call | solution.py:358
  61.2 1.9 %hand_on.1 = (bf16[1376,128]{1,0:T(8,128)(2,1)}, f32[16,1376]{1,0:T(8,128)}, f32[16,1376]{1,0:T(8,128)}) custom-call(bf16[1376,128]{1,0:T(8,128)(2,1)} %get-tuple-element.9.up_in, f32[16,1376]{1,0:T(8,128)} %get-tuple-element.10.nf_in, f32[16,1376]{1,0:T(8,128)} %get-tuple-element.11.ns_in), custom_call_target="tpu_custom_call" | custom-call | tf_op jit(solution)/shard_map/hand_on/pallas_call | solution.py:368

commit v3 on v0

v3 whole, which is shorter than its diff:
```python
import jax
import jax.numpy as jnp
from jax import lax
from jax.experimental import pallas as pl
from jax.experimental.pallas import tpu as pltpu
from jax.sharding import PartitionSpec as P

STEP = 10
MESH = pl.DeviceIdType.MESH
NX, NY, NZ = 4, 4, 4
KC = 4

TURN = (0, 3, 1, 2)
CUTS = (1, 1, 1, 2)

ORDER = (
    "P10", "P11", "P12", "P20", "P13", "P21", "P22", "U00", "U10", "U01", "P23", "U11", "U02", "U20", "U12", "U21",
    "U03", "U04", "U30", "U13", "U14", "U22", "U31", "U40", "U23", "U24", "U32", "U41", "U33", "U34", "U42", "U43", "U44",
    "U50", "U52", "U51", "U60", "U53", "U54", "U62", "U61", "U63", "U64",
)


def units(ff):
    made = []
    for i, k in enumerate(TURN):
        step = -(-ff // (128 * CUTS[i])) * 128
        made += [(k, h, h * step, min(ff, (h + 1) * step)) for h in range(CUTS[i])]
    return made


def kernel(
    a_hbm, g_hbm, s_hbm, m_hbm, v_hbm,
    up_v, nf_v, ns_v,
    a_v, g_v, gt, s_v, b_v, m_v, v_v,
    xs, xo, xr, ho, zs, zr, pt, rf, cs, cr, ty, ys, yr, ws, wr, lr, acc,
    ld, xss, xrs, zss, zrs, xas, xar, css, crs, yss, yrs, wss, wrs, bss, brs, yas, yar, c2s, c2r,
):
    dp = lax.axis_index("dp")
    t = lax.axis_index("tensor")
    x, zh = t % NX, t // NX
    zl, y, c = dp // 8, (dp // 2) % NY, dp % 2
    f32, bf16 = jnp.float32, jnp.bfloat16
    rank = s_v.shape[1]
    ff = gt.shape[1]
    kr = rank // KC
    own = kr // (2 * NY)
    tb = a_v.shape[1]
    depth = s_v.shape[0]
    rows = b_v.shape[0]
    unit = units(ff)

    def x_at(d):
        return (dp, zh * NX + (x + d) % NX)

    def y_at(d):
        return (zl * 8 + ((y + d) % NY) * 2 + c, t)

    def z_at(k):
        return (k * 8 + y * 2 + c, t)

    z_far = (dp, (1 - zh) * NX + x)
    core = (dp + 1 - 2 * c, t)

    barrier = pltpu.get_barrier_semaphore()
    peers = [x_at(d) for d in range(1, NX)] + [y_at(d) for d in range(1, NY)]
    peers += [z_at((zl + d) % NZ) for d in range(1, NZ)] + [z_far, core]
    loads = [pltpu.make_async_copy(s_hbm.at[pl.ds(pl.multiple_of(t * depth, depth), depth)], s_v, ld.at[0])]
    for i, d in enumerate((1, 2, 3, 0)):
        at = pl.multiple_of(((x + d) % NX) * tb, tb)
        loads.append(pltpu.make_async_copy(a_hbm.at[pl.ds(at, tb)], a_v.at[d], ld.at[1 + i]))
    for d in range(NX):
        at = pl.multiple_of(((x + NX - d) % NX) * tb, tb)
        loads.append(pltpu.make_async_copy(g_hbm.at[:, pl.ds(at, tb)], g_v.at[:, pl.ds(d * tb, tb)], ld.at[5 + d]))
    loads.append(pltpu.make_async_copy(m_hbm, m_v, ld.at[9]))
    loads.append(pltpu.make_async_copy(v_hbm, v_v, ld.at[10]))
    loads.append(pltpu.make_async_copy(s_hbm.at[pl.ds(pl.multiple_of(dp * rows, rows), rows)], b_v, ld.at[11]))
    for load in loads[:5]:
        load.start()
    for peer in peers:
        pl.semaphore_signal(barrier, inc=1, device_id=peer, device_id_type=MESH)

    def remote(src, dst, send, recv, to):
        return pltpu.make_async_remote_copy(
            src_ref=src, dst_ref=dst, send_sem=send, recv_sem=recv, device_id=to, device_id_type=MESH
        )

    def span(k):
        return slice(k * kr, (k + 1) * kr)

    def rows_of(k):
        return pl.ds(k * kr, kr)

    def slot(d):
        return pl.ds(d * tb, tb)

    def x_copy(k, d):
        r = rows_of(k)
        return remote(xs.at[d - 1, r], xr.at[d - 1, r], xss.at[k, d - 1], xrs.at[k, d - 1], x_at(d))

    def z_copy(k):
        r = rows_of(k)
        return remote(zs.at[r], zr.at[r], zss.at[k], zrs.at[k], z_far)

    def xa_copy(k, d):
        src, dst = pt.at[k, :, :, :, slot(0)], pt.at[k, :, :, :, slot(d)]
        return remote(src, dst, xas.at[k, d - 1], xar.at[k, d - 1], x_at(d))

    def project(k, d):
        return lax.dot_general(s_v[:, span(k)], a_v[d], (((0,), (1,)), ((), ())), preferred_element_type=f32)

    def send_partial(k):
        first = k == TURN[0]
        if first:
            loads[0].wait()
        for d in (2, 1, 3):
            if first:
                loads[d].wait()
            xs[d - 1, span(k)] = project(k, d).astype(bf16)
            if first and d == 2:
                pl.semaphore_wait(barrier, len(peers))
            x_copy(k, d).start()
        if first:
            for load in loads[5:]:
                load.start()
            loads[4].wait()
        xo[span(k)] = project(k, 0)

    def turn_g():
        for d in range(NX):
            loads[5 + d].wait()
            gt[d * tb : (d + 1) * tb] = g_v[:, d * tb : (d + 1) * tb].T

    def piece1(i):
        k = TURN[i]
        r = span(k)
        for d in (1, 3, 2):
            x_copy(k, d).wait_recv()
        h = xo[r] + xr[0, r].astype(f32) + xr[1, r].astype(f32) + xr[2, r].astype(f32)
        zs[r] = h.astype(bf16)
        z_copy(k).start()
        ho[r] = h

    def piece2(i):
        k = TURN[i]
        r = span(k)
        z_copy(k).wait_recv()
        pt[k, :, :, :, 0:tb] = (ho[r] + zr[r].astype(f32)).astype(bf16).reshape(NY, 2, own, tb)
        for d in (2, 1, 3):
            xa_copy(k, d).start()

    def cols(u):
        return pl.ds(unit[u][2], unit[u][3] - unit[u][2])

    def c_copy(u):
        k = unit[u][0]
        return remote(cs.at[k, :, :, cols(u)], cr.at[k, :, :, cols(u)], css.at[u], crs.at[u], core)

    def y_copy(u, d):
        k = unit[u][0]
        src, dst = ys.at[k, (y + d) % NY, :, cols(u)], yr.at[k, d - 1, :, cols(u)]
        return remote(src, dst, yss.at[u, d - 1], yrs.at[u, d - 1], y_at(d))

    def w_copy(u):
        k, h = unit[u][:2]
        place = (zl - k + NZ - 1) % NZ
        return remote(ws.at[k, :, cols(u)], wr.at[place, :, cols(u)], wss.at[u], wrs.at[h, place], z_at(k))

    def w_wait(u, d):
        k, h = unit[u][:2]
        theirs = wr.at[d - 1, :, cols(u)]
        remote(theirs, theirs, wss.at[u], wrs.at[h, d - 1], z_at((k + d) % NZ)).wait_recv()

    def b_copy(u, d):
        k, h = unit[u][:2]
        mine = lr.at[k, y, c, :, cols(u)]
        return remote(mine, mine, bss.at[h, d - 1], brs.at[u], z_at((k + d) % NZ))

    def ya_copy(u, d):
        mine = lr.at[unit[u][0], y, c, :, cols(u)]
        return remote(mine, mine, yas.at[u, d - 1], yar.at[u, d - 1], y_at(d))

    def ya_wait(u, d):
        theirs = lr.at[unit[u][0], (y + NY - d) % NY, c, :, cols(u)]
        remote(theirs, theirs, yas.at[u, d - 1], yar.at[u, d - 1], y_at(d)).wait_recv()

    def c2_copy(u, d):
        mine = lr.at[unit[u][0], (y + NY - d) % NY, c, :, cols(u)]
        return remote(mine, mine, c2s.at[u, d], c2r.at[u, d], core)

    def c2_wait(u, d):
        theirs = lr.at[unit[u][0], (y + NY - d) % NY, 1 - c, :, cols(u)]
        remote(theirs, theirs, c2s.at[u, d], c2r.at[u, d], core).wait_recv()

    def unit0(u):
        k, h, lo, hi = unit[u]
        if h == 0:
            for d in (1, 3, 2):
                xa_copy(k, d).wait_recv()

        def product(parity):
            p = pt[k, :, parity].reshape(NY * own, pt.shape[-1])
            return jnp.dot(p, gt[:, lo:hi], preferred_element_type=f32).reshape(NY, own, hi - lo)

        cs[k, :, :, lo:hi] = product(1 - c).astype(bf16)
        c_copy(u).start()
        rf[k, :, :, lo:hi] = product(c)

    def unit1(u):
        k, h, lo, hi = unit[u]
        c_copy(u).wait_recv()
        both = rf[k, :, :, lo:hi] + cr[k, :, :, lo:hi].astype(f32)
        ys[k, :, :, lo:hi] = both.astype(bf16)
        for d in (2, 1, 3):
            y_copy(u, d).start()
        ty[k, :, :, lo:hi] = both

    def unit2(u):
        k, h, lo, hi = unit[u]
        for d in (1, 3, 2):
            y_copy(u, d).wait_recv()
        total = ty[k, y, :, lo:hi]
        for d in (1, 2, 3):
            total = total + yr[k, d - 1, :, lo:hi].astype(f32)
        ty[k, y, :, lo:hi] = total

        @pl.when(zl != k)
        def _():
            ws[k, :, lo:hi] = total.astype(bf16)
            w_copy(u).start()

    def far_first(k):
        return sorted((1, 2, 3), key=lambda d: -abs((k + d) % NZ - k))

    def unit3(u):
        k, h, lo, hi = unit[u]

        @pl.when(zl == k)
        def _():
            for d in (1, 2, 3):
                w_wait(u, d)
            if h == 0:
                loads[9].wait()
                loads[10].wait()
            reduced = ty[k, y, :, lo:hi]
            for d in (1, 2, 3):
                reduced = reduced + wr[d - 1, :, lo:hi].astype(f32)
            first, second = m_v[:, lo:hi], v_v[:, lo:hi]
            first_hat = (0.9 / (1.0 - 0.9**STEP)) * first + (0.1 / (1.0 - 0.9**STEP)) * reduced
            second_hat = (0.999 / (1.0 - 0.999**STEP)) * second + (0.001 / (1.0 - 0.999**STEP)) * reduced * reduced
            lr[k, y, c, :, lo:hi] = (first_hat / (jnp.sqrt(second_hat) + 1e-08)).astype(bf16)
            for d in far_first(k):
                b_copy(u, d).start()
            nf_v[:, lo:hi] = 0.9 * first + 0.1 * reduced
            ns_v[:, lo:hi] = 0.999 * second + 0.001 * reduced * reduced

    def unit4(u):
        @pl.when(zl != unit[u][0])
        def _():
            b_copy(u, 1).wait_recv()

        for d in (2, 1, 3):
            ya_copy(u, d).start()
        c2_copy(u, 0).start()

    def unit5(u):
        for d in (1, 3, 2):
            ya_wait(u, d)
            c2_copy(u, d).start()

    def unit6(u):
        k, h, lo, hi = unit[u]
        for d in (0, 1, 3, 2):
            c2_wait(u, d)
        if u == 0:
            loads[11].wait()
        low = lr[k, :, :, :, lo:hi].reshape(kr, hi - lo)
        part = lax.dot_general(
            low, b_v[:, k * kr : (k + 1) * kr], (((0,), (1,)), ((), ())), preferred_element_type=f32
        )
        if k == TURN[0]:
            acc[lo:hi] = part
        elif k != TURN[-1]:
            acc[lo:hi] += part
        else:
            up_v[lo:hi] = (acc[lo:hi] + part).astype(bf16)

    for k in TURN:
        send_partial(k)
    turn_g()
    stages = dict(P=(None, piece1, piece2), U=(unit0, unit1, unit2, unit3, unit4, unit5, unit6))
    for name in ORDER:
        stages[name[0]][int(name[1])](int(name[2]))

    for k in TURN:
        for d in (1, 2, 3):
            x_copy(k, d).wait_send()
            xa_copy(k, d).wait_send()
        z_copy(k).wait_send()
    for u, (k, h, _, _) in enumerate(unit):
        c_copy(u).wait_send()
        for d in (1, 2, 3):
            y_copy(u, d).wait_send()
            ya_copy(u, d).wait_send()
        for d in range(NY):
            c2_copy(u, d).wait_send()

        @pl.when(zl != k)
        def _():
            w_copy(u).wait_send()

        @pl.when(zl == k)
        def _():
            for d in (1, 2, 3):
                b_copy(u, d).wait_send()


def hand_on(up_in, nf_in, ns_in, up_out, nf_out, ns_out, sem):
    pairs = ((up_in, up_out), (nf_in, nf_out), (ns_in, ns_out))
    writes = [pltpu.make_async_copy(src, dst, sem.at[i]) for i, (src, dst) in enumerate(pairs)]
    for write in writes:
        write.start()
    for write in writes:
        write.wait()


def local(activations, grad_out, subspace, first_moment, second_moment):
    tokens, depth = activations.shape
    ff = grad_out.shape[1]
    rank = subspace.shape[1]
    own = first_moment.shape[0]
    rows = subspace.shape[0] // lax.axis_size("dp")
    tb = tokens // NX
    kr = rank // KC
    f32, bf16 = jnp.float32, jnp.bfloat16
    dma = pltpu.SemaphoreType.DMA
    anywhere = pl.BlockSpec(memory_space=pl.ANY)
    scratch = [
        ((NX, tb, depth), bf16),
        ((ff, tokens), bf16),
        ((tokens, ff), bf16),
        ((depth, rank), bf16),
        ((rows, rank), bf16),
        ((own, ff), f32),
        ((own, ff), f32),
        ((NX - 1, rank, tb), bf16),
        ((rank, tb), f32),
        ((NX - 1, rank, tb), bf16),
        ((rank, tb), f32),
        ((rank, tb), bf16),
        ((rank, tb), bf16),
        ((KC, NY, 2, own, tokens), bf16),
        ((KC, NY, own, ff), f32),
        ((KC, NY, own, ff), bf16),
        ((KC, NY, own, ff), bf16),
        ((KC, NY, own, ff), f32),
        ((KC, NY, own, ff), bf16),
        ((KC, NY - 1, own, ff), bf16),
        ((KC, own, ff), bf16),
        ((NZ - 1, own, ff), bf16),
        ((KC, NY, 2, own, ff), bf16),
        ((ff, rows), f32),
    ]
    nu, nh = len(units(ff)), max(CUTS)
    sems = [(12,), (KC, 3), (KC, 3), (KC,), (KC,), (KC, 3), (KC, 3)]
    sems += [(nu,), (nu,), (nu, 3), (nu, 3), (nu,), (nh, 3), (nh, 3), (nu,), (nu, 3), (nu, 3), (nu, NY), (nu, NY)]
    flops = 2 * tokens * rank * (depth + ff) + 2 * rows * rank * ff
    shapes = (
        jax.ShapeDtypeStruct((ff, rows), bf16),
        jax.ShapeDtypeStruct((own, ff), f32),
        jax.ShapeDtypeStruct((own, ff), f32),
    )
    made = pl.pallas_call(
        kernel,
        out_shape=tuple(pltpu.VMEM(out.shape, out.dtype) for out in shapes),
        in_specs=[anywhere] * 5,
        out_specs=(pl.BlockSpec(memory_space=pltpu.VMEM),) * 3,
        scratch_shapes=[pltpu.VMEM(shape, dtype) for shape, dtype in scratch] + [dma(shape) for shape in sems],
        compiler_params=pltpu.CompilerParams(collective_id=0, has_side_effects=True, vmem_limit_bytes=56 << 20),
        cost_estimate=pl.CostEstimate(flops=flops, bytes_accessed=8 << 20, transcendentals=own * ff),
        name="galore",
    )(activations, grad_out.T, subspace, first_moment, second_moment)
    update, new_first, new_second = pl.pallas_call(
        hand_on,
        out_shape=shapes,
        in_specs=[anywhere] * 3,
        out_specs=(anywhere,) * 3,
        scratch_shapes=[dma((3,))],
        name="hand_on",
    )(*[pltpu.with_memory_space_constraint(one, pltpu.VMEM) for one in made])
    return update.T, new_first, new_second


def solution(mesh):
    in_specs = (P("dp", "tensor"), P("dp", "tensor"), P(), P("dp", "tensor"), P("dp", "tensor"))
    out_specs = (P("dp", "tensor"), P("dp", "tensor"), P("dp", "tensor"))
    return jax.shard_map(local, mesh=mesh, in_specs=in_specs, out_specs=out_specs, check_vma=False)
```

time: 422 us -> 60.4 us (0.14)
  waiting for transfers between devices: 391 us -> 0 us
  Pallas kernels: 0 us -> 59.6 us
  matrix products: 15.2 us -> 0 us
  between operations: 13.8 us -> 0.64 us
    all_gather x2 -> x0, waiting for transfers between devices: 250 us -> none  [the longest x1 188 us: local(): lax.all_gather(activations, 'tensor', axis=1, tiled=True)]
    reduce_scatter x1 -> x0, waiting for transfers between devices: 140 us -> none  [local(): lax.psum_scatter(lax.dot_general(projected, grad_out, (((0,), (0,)), ((),...]
    pallas_call x0 -> x2, Pallas kernels: none -> 59.6 us  [the longest x1 58.8 us: local(): pl.pallas_call(kernel, out_shape=tuple((pltpu.VMEM(out.shape, out.dtype)...]
    dot_general x2 -> x0, matrix products: 15.2 us -> none  [the longest x1 12.4 us: local(): lax.dot_general(projected, grad_out, (((0,), (0,)), ((), ())), preferred_...]
  transfers between devices with their start and end apart: 3 -> 0, of which waited for: 3 -> 0; matrix products, arithmetic and copies ran while one was open for 0% -> 0% of each run, Pallas kernels for 0% -> 0%
where the time goes in v3:
time: 60.4 us; the launch traced here: 60.3 us
  Pallas kernels  59.6 us (99%)
  between operations  0.64 us (1%)
    pallas_call x1, Pallas kernels, local(): pl.pallas_call(kernel, out_shape=tuple((pltpu.VMEM(out.shape, out.dtype)...  58.8 us

profile of v3, /device:TPU:1, one launch (start us, length us, event | category | flops | bytes accessed | tf_op | source)
XLA Modules:
  0.0 60.3 jit_solution(3881944059286142257)
XLA Ops:
  0.6 58.8 %galore.1 = (bf16[1376,128]{1,0:T(8,128)(2,1)S(1)}, f32[16,1376]{1,0:T(8,128)S(1)}, f32[16,1376]{1,0:T(8,128)S(1)}) custom-call(bf16[1024,512]{1,0:T(8,128)(2,1)} %a_hbm.1, bf16[1376,1024]{1,0:T(8,128)(2,1)} %bitcast.2, bf16[4096,512]{1,0:T(8,128)(2,1)} %s_hbm.1, f32[16,1376]{1,0:T(8,128)} %m_hbm.1, f32[16,1376]{1,0:T(8,128)} %v_hbm.1), custom_call_target="tpu_custom_call" | custom-call | flops 2160066560 | bytes 8388608 | tf_op jit(solution)/shard_map/galore/pallas_call | solution.py:372
  59.5 0.8 %hand_on.1 = (bf16[1376,128]{1,0:T(8,128)(2,1)}, f32[16,1376]{1,0:T(8,128)}, f32[16,1376]{1,0:T(8,128)}) custom-call(bf16[1376,128]{1,0:T(8,128)(2,1)S(1)} %get-tuple-element.9.up_in, f32[16,1376]{1,0:T(8,128)S(1)} %get-tuple-element.10.nf_in, f32[16,1376]{1,0:T(8,128)S(1)} %get-tuple-element.11.ns_in), custom_call_target="tpu_custom_call" | custom-call | tf_op jit(solution)/shard_map/hand_on/pallas_call | solution.py:382

commit v4 on v3

--- a/solution.py
+++ b/solution.py
@@ -10,7 +10,7 @@
 NX, NY, NZ = 4, 4, 4
 KC = 4
 
-TURN = (0, 3, 1, 2)
+TURN = (3, 1, 2, 0)
 CUTS = (1, 1, 1, 2)
 
 ORDER = (

time: 60.4 us -> 59.3 us (0.982)
  Pallas kernels: 59.6 us -> 58.6 us
    pallas_call x1, Pallas kernels: 58.8 us -> 57.8 us  [local(): pl.pallas_call(kernel, out_shape=tuple((pltpu.VMEM(out.shape, out.dtype)...]
where the time goes in v4:
time: 59.3 us; the launch traced here: 59.2 us
  Pallas kernels  58.6 us (99%)
  between operations  0.64 us (1%)
    pallas_call x1, Pallas kernels, local(): pl.pallas_call(kernel, out_shape=tuple((pltpu.VMEM(out.shape, out.dtype)...  57.8 us

profile of v4, /device:TPU:1, one launch (start us, length us, event | category | flops | bytes accessed | tf_op | source)
XLA Modules:
  0.0 59.2 jit_solution(7501029292600620894)
XLA Ops:
  0.6 57.8 %galore.1 = (bf16[1376,128]{1,0:T(8,128)(2,1)S(1)}, f32[16,1376]{1,0:T(8,128)S(1)}, f32[16,1376]{1,0:T(8,128)S(1)}) custom-call(bf16[1024,512]{1,0:T(8,128)(2,1)} %a_hbm.1, bf16[1376,1024]{1,0:T(8,128)(2,1)} %bitcast.2, bf16[4096,512]{1,0:T(8,128)(2,1)} %s_hbm.1, f32[16,1376]{1,0:T(8,128)} %m_hbm.1, f32[16,1376]{1,0:T(8,128)} %v_hbm.1), custom_call_target="tpu_custom_call" | custom-call | flops 2160066560 | bytes 8388608 | tf_op jit(solution)/shard_map/galore/pallas_call | solution.py:372
  58.4 0.8 %hand_on.1 = (bf16[1376,128]{1,0:T(8,128)(2,1)}, f32[16,1376]{1,0:T(8,128)}, f32[16,1376]{1,0:T(8,128)}) custom-call(bf16[1376,128]{1,0:T(8,128)(2,1)S(1)} %get-tuple-element.9.up_in, f32[16,1376]{1,0:T(8,128)S(1)} %get-tuple-element.10.nf_in, f32[16,1376]{1,0:T(8,128)S(1)} %get-tuple-element.11.ns_in), custom_call_target="tpu_custom_call" | custom-call | tf_op jit(solution)/shard_map/hand_on/pallas_call | solution.py:382

commit v5 on v4

--- a/solution.py
+++ b/solution.py
@@ -15,8 +15,8 @@
 
 ORDER = (
     "P10", "P11", "P12", "P20", "P13", "P21", "P22", "U00", "U10", "U01", "P23", "U11", "U02", "U20", "U12", "U21",
-    "U03", "U04", "U30", "U13", "U14", "U22", "U31", "U40", "U23", "U24", "U32", "U41", "U33", "U34", "U42", "U43", "U44",
-    "U50", "U52", "U51", "U60", "U53", "U54", "U62", "U61", "U63", "U64",
+    "U03", "U04", "U30", "U13", "U14", "U22", "U31", "U40", "U23", "U24", "U32", "U41", "U33", "U34", "U50", "U42", "U51",
+    "U43", "U44", "U60", "U61", "U52", "U53", "U54", "U62", "U63", "U64",
 )
 
 
@@ -208,25 +208,58 @@
     def unit1(u):
         k, h, lo, hi = unit[u]
         c_copy(u).wait_recv()
-        both = rf[k, :, :, lo:hi] + cr[k, :, :, lo:hi].astype(f32)
-        ys[k, :, :, lo:hi] = both.astype(bf16)
-        for d in (2, 1, 3):
-            y_copy(u, d).start()
-        ty[k, :, :, lo:hi] = both
+        for d in (2, 1, 3, 0):
+            yy = (y + d) % NY
+            both = rf[k, yy, :, lo:hi] + cr[k, yy, :, lo:hi].astype(f32)
+            if d:
+                ys[k, yy, :, lo:hi] = both.astype(bf16)
+                y_copy(u, d).start()
+            else:
+                ty[k, :, lo:hi] = both
 
     def unit2(u):
         k, h, lo, hi = unit[u]
         for d in (1, 3, 2):
             y_copy(u, d).wait_recv()
-        total = ty[k, y, :, lo:hi]
+        total = ty[k, :, lo:hi]
         for d in (1, 2, 3):
             total = total + yr[k, d - 1, :, lo:hi].astype(f32)
-        ty[k, y, :, lo:hi] = total
+        ty[k, :, lo:hi] = total
 
         @pl.when(zl != k)
         def _():
             ws[k, :, lo:hi] = total.astype(bf16)
             w_copy(u).start()
+
+        if h == 0:
+            sent_first(k)
+
+    def sent_first(k):
+        for d in (1, 2, 3):
+            x_copy(k, d).wait_send()
+            xa_copy(k, d).wait_send()
+        z_copy(k).wait_send()
+
+    def sent_sums(u):
+        c_copy(u).wait_send()
+        for d in (1, 2, 3):
+            y_copy(u, d).wait_send()
+
+        @pl.when(zl != unit[u][0])
+        def _():
+            w_copy(u).wait_send()
+
+    def sent_steps(u):
+        @pl.when(zl == unit[u][0])
+        def _():
+            for d in (1, 2, 3):
+                b_copy(u, d).wait_send()
+
+    def sent_gathered(u):
+        for d in (1, 2, 3):
+            ya_copy(u, d).wait_send()
+        for d in range(NY):
+            c2_copy(u, d).wait_send()
 
     def far_first(k):
         return sorted((1, 2, 3), key=lambda d: -abs((k + d) % NZ - k))
@@ -241,7 +274,7 @@
             if h == 0:
                 loads[9].wait()
                 loads[10].wait()
-            reduced = ty[k, y, :, lo:hi]
+            reduced = ty[k, :, lo:hi]
             for d in (1, 2, 3):
                 reduced = reduced + wr[d - 1, :, lo:hi].astype(f32)
             first, second = m_v[:, lo:hi], v_v[:, lo:hi]
@@ -261,11 +294,13 @@
         for d in (2, 1, 3):
             ya_copy(u, d).start()
         c2_copy(u, 0).start()
+        sent_sums(u)
 
     def unit5(u):
         for d in (1, 3, 2):
             ya_wait(u, d)
             c2_copy(u, d).start()
+        sent_steps(u)
 
     def unit6(u):
         k, h, lo, hi = unit[u]
@@ -283,6 +318,7 @@
             acc[lo:hi] += part
         else:
             up_v[lo:hi] = (acc[lo:hi] + part).astype(bf16)
+        sent_gathered(u)
 
     for k in TURN:
         send_partial(k)
@@ -290,28 +326,6 @@
     stages = dict(P=(None, piece1, piece2), U=(unit0, unit1, unit2, unit3, unit4, unit5, unit6))
     for name in ORDER:
         stages[name[0]][int(name[1])](int(name[2]))
-
-    for k in TURN:
-        for d in (1, 2, 3):
-            x_copy(k, d).wait_send()
-            xa_copy(k, d).wait_send()
-        z_copy(k).wait_send()
-    for u, (k, h, _, _) in enumerate(unit):
-        c_copy(u).wait_send()
-        for d in (1, 2, 3):
-            y_copy(u, d).wait_send()
-            ya_copy(u, d).wait_send()
-        for d in range(NY):
-            c2_copy(u, d).wait_send()
-
-        @pl.when(zl != k)
-        def _():
-            w_copy(u).wait_send()
-
-        @pl.when(zl == k)
-        def _():
-            for d in (1, 2, 3):
-                b_copy(u, d).wait_send()
 
 
 def hand_on(up_in, nf_in, ns_in, up_out, nf_out, ns_out, sem):
@@ -352,7 +366,7 @@
         ((KC, NY, own, ff), f32),
         ((KC, NY, own, ff), bf16),
         ((KC, NY, own, ff), bf16),
-        ((KC, NY, own, ff), f32),
+        ((KC, own, ff), f32),
         ((KC, NY, own, ff), bf16),
         ((KC, NY - 1, own, ff), bf16),
         ((KC, own, ff), bf16),

time: 59.3 us -> 59.1 us (level)
  no operation moved by 1% of the time
where the time goes in v5:
time: 59.1 us; the launch traced here: 59 us
  Pallas kernels  58.4 us (99%)
  between operations  0.64 us (1%)
    pallas_call x1, Pallas kernels, local(): pl.pallas_call(kernel, out_shape=tuple((pltpu.VMEM(out.shape, out.dtype)...  57.6 us

profile of v5, /device:TPU:1, one launch (start us, length us, event | category | flops | bytes accessed | tf_op | source)
XLA Modules:
  0.0 59.0 jit_solution(6463566914291148050)
XLA Ops:
  0.6 57.6 %galore.1 = (bf16[1376,128]{1,0:T(8,128)(2,1)S(1)}, f32[16,1376]{1,0:T(8,128)S(1)}, f32[16,1376]{1,0:T(8,128)S(1)}) custom-call(bf16[1024,512]{1,0:T(8,128)(2,1)} %a_hbm.1, bf16[1376,1024]{1,0:T(8,128)(2,1)} %bitcast.2, bf16[4096,512]{1,0:T(8,128)(2,1)} %s_hbm.1, f32[16,1376]{1,0:T(8,128)} %m_hbm.1, f32[16,1376]{1,0:T(8,128)} %v_hbm.1), custom_call_target="tpu_custom_call" | custom-call | flops 2160066560 | bytes 8388608 | tf_op jit(solution)/shard_map/galore/pallas_call | solution.py:386
  58.2 0.8 %hand_on.1 = (bf16[1376,128]{1,0:T(8,128)(2,1)}, f32[16,1376]{1,0:T(8,128)}, f32[16,1376]{1,0:T(8,128)}) custom-call(bf16[1376,128]{1,0:T(8,128)(2,1)S(1)} %get-tuple-element.9.up_in, f32[16,1376]{1,0:T(8,128)S(1)} %get-tuple-element.10.nf_in, f32[16,1376]{1,0:T(8,128)S(1)} %get-tuple-element.11.ns_in), custom_call_target="tpu_custom_call" | custom-call | tf_op jit(solution)/shard_map/hand_on/pallas_call | solution.py:396
